TPU v7x, 32 devices: a whole 2x2x4 slice. The times are simulated.
32 devices in a mesh: row: 2 (over core), lat: 8 (over z, x), grp: 2 (over y).
Axes of the slice: x: 2, y: 2, z: 4, core: 2. Of those that a mesh axis runs over, the one named last changes fastest.
Arguments:
- stream_in: bfloat16 [192, 3584], P(('lat', 'grp'), 'row'), may hold values from -36 to 36, as said below
- pre_gain: float32 [3584], P('row'), may hold values from 0.25 to 1.75
- gate_weight: bfloat16 [3584, 14336], P('row', ('lat', 'grp')), may hold values from -0.09375 to 0.09375
- up_weight: bfloat16 [3584, 14336], P('row', ('lat', 'grp')), may hold values from -0.09375 to 0.09375
- down_weight: bfloat16 [14336, 3584], P(('lat', 'grp'), 'row'), may hold values from -0.046875 to 0.046875
- post_gain: float32 [3584], P('row'), may hold values from 0.25 to 1.75
- enc_weight: float32 [3584, 16384], P('row', ('lat', 'grp')), may hold values from -0.09375 to 0.09375
- enc_bias: float32 [16384], P(('lat', 'grp')), may hold values from -3 to 3
- dec_weight: float32 [16384, 3584], P(('lat', 'grp'), 'row'), may hold values from -0.046875 to 0.046875
- dec_bias: float32 [3584], P('row'), may hold values from -3 to 3
Outputs:
- stream_out: bfloat16 [192, 3584], P(('lat', 'grp'), 'row')
- grad_enc: float32 [3584, 16384], P('row', ('lat', 'grp'))
- grad_enc_bias: float32 [16384], P(('lat', 'grp'))
- grad_dec: float32 [16384, 3584], P(('lat', 'grp'), 'row')
- grad_dec_bias: float32 [3584], P('row')
Inputs may be any that keep to these rules, and one draw needn't show every extreme that they name: `stream_in`: Real-valued activations with scales that differ over rows and features.
All inputs are finite; a program needn't handle non-finite values.
Results may differ from a plain program's by a relative error of at most 0.013.
Values may be sent and summed in bfloat16 or wider, within the bound.
A program may use at most 128 MiB of HBM per device.

v0:
```python
import math

import jax
import jax.numpy as jnp
from jax import lax
from jax.sharding import PartitionSpec as P

D = 3584


epsilon = 1e-06
sparsity = 0.2
sharpness = 4.0


def smooth_relu(value):
    return jax.nn.softplus(sharpness * value) / sharpness


def activate(summed, hidden_width):
    return (
        jax.nn.gelu(summed[:, :hidden_width], approximate=True) * summed[:, hidden_width:]
    ).astype(jnp.bfloat16)


def body(
    stream_in,
    pre_gain,
    gate_weight,
    up_weight,
    down_weight,
    post_gain,
    enc_weight,
    enc_bias,
    dec_weight,
    dec_bias,
):
    highest = lax.Precision.HIGHEST
    stream = stream_in.astype(jnp.float32)
    hidden_width = gate_weight.shape[1]
    squares = lax.psum(jnp.sum(stream * stream, axis=1), "row")
    normed = (stream * lax.rsqrt(squares[:, None] / D + epsilon) * pre_gain).astype(jnp.bfloat16)
    joined = jnp.concatenate([gate_weight, up_weight], axis=1)
    partial_proj = jnp.dot(
        lax.all_gather(normed, ("lat", "grp"), axis=0, tiled=True),
        joined,
        preferred_element_type=jnp.float32,
    )
    shares = lax.psum_scatter(partial_proj, "row", scatter_dimension=0, tiled=True)
    hidden = lax.all_gather(activate(shares, hidden_width), "row", axis=0, tiled=True)
    output = lax.psum_scatter(
        jnp.dot(hidden, down_weight, preferred_element_type=jnp.float32),
        ("lat", "grp"),
        scatter_dimension=0,
        tiled=True,
    )
    out_squares = lax.psum(jnp.sum(output * output, axis=1), "row")
    stream_out = (
        stream + output * lax.rsqrt(out_squares[:, None] / D + epsilon) * post_gain
    ).astype(jnp.bfloat16)
    relayed = lax.all_gather(stream_out, ("lat", "grp"), axis=0, tiled=True)
    inputs = relayed.astype(jnp.float32)
    scale = 1.0 / math.sqrt(inputs.shape[0])
    encoded = jnp.dot(inputs, enc_weight, precision=highest, preferred_element_type=jnp.float32)
    preact = lax.psum(encoded, "row") + enc_bias
    latents = smooth_relu(preact)
    partial_rec = jnp.dot(
        latents, dec_weight, precision=highest, preferred_element_type=jnp.float32
    )
    recon = lax.psum(partial_rec, ("lat", "grp"))
    residual_grad = (recon + dec_bias - inputs) * scale
    grad_dec = jnp.dot(
        latents.T, residual_grad, precision=highest, preferred_element_type=jnp.float32
    )
    grad_dec_bias = jnp.sum(residual_grad, axis=0)
    back_term = jnp.dot(
        residual_grad, dec_weight.T, precision=highest, preferred_element_type=jnp.float32
    )
    latent_grad = (
        lax.psum(back_term.astype(jnp.bfloat16), "row").astype(jnp.float32) + sparsity * scale
    )
    preact_grad = latent_grad * jax.nn.sigmoid(sharpness * preact)
    grad_enc = jnp.dot(inputs.T, preact_grad, precision=highest, preferred_element_type=jnp.float32)
    grad_enc_bias = jnp.sum(preact_grad, axis=0)
    return (stream_out, grad_enc, grad_enc_bias, grad_dec, grad_dec_bias)


def solution(mesh):
    placed = (
        P(("lat", "grp"), "row"),
        P("row"),
        P("row", ("lat", "grp")),
        P("row", ("lat", "grp")),
        P(("lat", "grp"), "row"),
        P("row"),
        P("row", ("lat", "grp")),
        P(("lat", "grp")),
        P(("lat", "grp"), "row"),
        P("row"),
    )
    return jax.shard_map(
        body,
        mesh=mesh,
        in_specs=placed,
        out_specs=(
            P(("lat", "grp"), "row"),
            P("row", ("lat", "grp")),
            P(("lat", "grp")),
            P(("lat", "grp"), "row"),
            P("row"),
        ),
        check_vma=False,
    )
```

profile of v0, /device:TPU:0, one launch (start us, length us, event | category | flops | bytes accessed | tf_op | source)
XLA Modules:
  0.0 402.0 jit_solution(2031803251081122726)
XLA Ops:
  7.2 0.0 copy-start
  7.2 0.0 reduce-scatter.4.cloned.1.call-start
  7.2 1.1 fusion.20
  8.3 2.6 psum.35
  10.9 0.9 fusion.24
  11.8 50.0 %all-gather = bf16[16,12,1792]{2,1,0:T(8,128)(2,1)} all-gather(bf16[1,12,1792]{2,1,0:T(8,128)(2,1)S(1)} %fusion.24), channel_id=1, replica_groups=mesh['row'=2,'lat'=8,'grp'=2] {'lat','grp'}, dimensions={0}, use_global_device_ids=true | all-gather | bytes 731136 | tf_op jit(solution)/shard_map/all_gather | solution.py:45
  61.9 2.1 reshape.23
  63.9 5.6 %fusion.1 = f32[192,1792]{1,0:T(8,128)} fusion(bf16[192,1792]{1,0:T(8,128)(2,1)} %reshape.23, bf16[1792,896]{1,0:T(8,128)(2,1)} %param.13, bf16[1792,896]{1,0:T(8,128)(2,1)} %param.12), kind=kOutput, calls=%fused_computation | convolution fusion | flops 1245970432 | bytes 8486912 | tf_op jit(solution)/shard_map/dot_general | solution.py:44
  69.5 0.0 reduce-scatter.4.cloned.1.call-update
  69.6 0.0 all-reduce.6.cloned.1.call-start
  69.6 4.8 %reduce-scatter.4.cloned.1.call-done = f32[96,1792]{1,0:T(8,128)} async-done(((f32[192,1792]{1,0:T(8,128)}), f32[96,1792]{1,0:T(8,128)}) %reduce-scatter.4.cloned.1.call-update) | async-done | bytes 688144 | tf_op jit(solution)/shard_map/reduce_scatter | solution.py:49
  74.4 1.2 fusion.14
  75.6 2.1 all_gather.10
  77.7 2.0 fusion.36
  79.6 52.9 %fusion = f32[16,1792]{1,0:T(8,128)S(1)} fusion(f32[192,1792]{1,0:T(8,128)} %fusion.36), kind=kCustom, calls=%all-reduce-scatter | all-reduce-scatter fusion | flops 458753 | bytes 1491456
  132.6 1.3 collective-permute-start.2
  133.9 4.5 %collective-permute-start.1 = (f32[16,1792]{1,0:T(8,128)S(1)}, f32[16,1792]{1,0:T(8,128)}, u32[]{:S(2)}, u32[]{:S(2)}) collective-permute-start(f32[16,1792]{1,0:T(8,128)S(1)} %fusion), channel_id=1, source_target_pairs={{0,2},{1,3},{2,4},{3,5},{4,6},{5,7},{6,8},{7,9},{8,10},{9,11},{10,... | collective-permute-start | bytes 344072
  138.4 2.2 collective-permute-start
  140.5 0.7 slice.10
  141.2 2.4 collective-permute-start.3
  143.6 0.6 dynamic-slice.4
  144.8 0.8 collective-permute-done.3
  145.6 0.0 collective-permute-done.2
  145.6 0.0 collective-permute-done.1
  145.6 8.0 %concatenate.4 = f32[76,1792]{1,0:T(8,128)} concatenate(f32[12,1792]{1,0:T(8,128)} %collective-permute-done.3, f32[16,1792]{1,0:T(8,128)S(1)} %collective-permute-done.2, f32[16,1792]{1,0:T(8,128)} %collective-permute-done.1, f32[16,1792]{1,0:T(8,128)} %collective-permute-done, f32[16,1792]{1,0:T(8,128)S(1)} %fusion), dimensions={0} | concatenate | bytes 1089536
  153.6 1.0 multiply_reduce_fusion
  154.6 2.5 psum.36
  157.1 1.0 fusion.23
  158.1 0.0 copy-start.5
  158.2 47.7 %all-gather.1 = bf16[16,12,1792]{2,1,0:T(8,128)(2,1)} all-gather(bf16[1,12,1792]{2,1,0:T(8,128)(2,1)S(1)} %bitcast.14), channel_id=1, replica_groups=mesh['row'=2,'lat'=8,'grp'=2] {'lat','grp'}, dimensions={0}, use_global_device_ids=true | all-gather | bytes 731136 | tf_op jit(solution)/shard_map/all_gather | solution.py:61
  205.8 2.1 reshape.25
  207.9 7.3 %fusion.37 = f32[192,1024]{1,0:T(8,128)} fusion(bf16[192,1792]{1,0:T(8,128)(2,1)} %reshape.25, f32[1792,1024]{1,0:T(8,128)} %param.16), kind=kOutput, calls=%fused_computation.46 | convolution fusion | flops 4227858432 | bytes 8814592 | tf_op jit(solution)/shard_map/dot_general | solution.py:64
  215.2 0.0 all-reduce.6.cloned.1.call-update
  215.3 0.0 copy-start.7
  215.3 0.2 all-reduce.8.cloned.1.call-start
  215.5 15.0 %all-reduce.6.cloned.1.call-done = f32[192,1024]{1,0:T(8,128)} async-done(((f32[192,1024]{1,0:T(8,128)}), f32[192,1024]{1,0:T(8,128)}) %all-reduce.6.cloned.1.call-update) | async-done | bytes 786448 | tf_op jit(solution)/shard_map/psum | solution.py:65
  230.5 9.9 %fusion.17 = f32[192,1792]{1,0:T(8,128)} fusion(f32[1024,1792]{1,0:T(8,128)} %param.18, f32[192,1024]{1,0:T(8,128)} %all-reduce.6.cloned.1.call-done, f32[1024]{0:T(1024)S(1)} %copy-done.6), kind=kOutput, calls=%fused_computation.21 | convolution fusion | flops 4229627904 | bytes 9506816 | tf_op jit(solution)/shard_map/dot_general | solution.py:67
  240.4 0.0 all-reduce.8.cloned.1.call-update
  240.4 0.3 all-reduce.10.cloned.1.call-start
  240.7 116.4 %all-reduce.8.cloned.1.call-done = f32[192,1792]{1,0:T(8,128)} async-done(((f32[192,1792]{1,0:T(8,128)}), f32[192,1792]{1,0:T(8,128)}) %all-reduce.8.cloned.1.call-update) | async-done | bytes 1376272 | tf_op jit(solution)/shard_map/psum | solution.py:70
  357.0 12.0 %convolution_convert_fusion = bf16[192,1024]{1,0:T(8,128)(2,1)} fusion(f32[1024,1792]{1,0:T(8,128)} %param.18, bf16[192,1792]{1,0:T(8,128)(2,1)} %reshape.25, f32[192,1792]{1,0:T(8,128)} %all-reduce.8.cloned.1.call-done, f32[1792]{0:T(1024)S(1)} %copy-done.7), kind=kOutput, calls=%fused_computation.6 | convolution fusion | flops 4229431296 | bytes 9804800 | tf_op jit(solution)/shard_map/dot_general | solution.py:76
  369.0 0.0 all-reduce.10.cloned.1.call-update
  369.0 0.0 copy-start.1
  369.0 2.5 fusion.19
  371.5 10.1 %fusion.15 = f32[1024,1792]{1,0:T(8,128)} fusion(f32[192,1024]{1,0:T(8,128)S(1)} %copy-done.3, f32[1024]{0:T(1024)S(1)} %copy-done.6, bf16[192,1792]{1,0:T(8,128)(2,1)S(1)} %copy-done.1, f32[192,1792]{1,0:T(8,128)} %all-reduce.8.cloned.1.call-done, f32[1792]{0:T(1024)S(1)} %copy-done.7), kind=kOutput, calls=%fused_computation.20 | convolution fusion | flops 4231004160 | bytes 10202112 | tf_op jit(solution)/shard_map/dot_general | solution.py:72
  381.6 5.0 %all-reduce.10.cloned.1.call-done = bf16[192,1024]{1,0:T(8,128)(2,1)} async-done(((bf16[192,1024]{1,0:T(8,128)(2,1)}), bf16[192,1024]{1,0:T(8,128)(2,1)}) %all-reduce.10.cloned.1.call-update) | async-done | bytes 393232 | tf_op jit(solution)/shard_map/psum | solution.py:80
  386.6 2.2 fusion.34
  388.8 6.7 %fusion.35 = f32[1792,1024]{1,0:T(8,128)} fusion(bf16[192,1792]{1,0:T(8,128)(2,1)S(1)} %copy-done.2, bf16[192,1024]{1,0:T(8,128)(2,1)} %all-reduce.10.cloned.1.call-done, f32[192,1024]{1,0:T(8,128)} %all-reduce.6.cloned.1.call-done, f32[1024]{0:T(1024)S(1)} %copy-done.6), kind=kOutput, calls=%fused_computation.44 | convolution fusion | flops 4229431296 | bytes 9211904 | tf_op jit(solution)/shard_map/dot_general | solution.py:83
  (19 shorter events, 0.1 us)
Async XLA Ops:
  7.2 70.5 %copy-start = (bf16[896,1792]{1,0:T(8,128)(2,1)S(1)}, bf16[896,1792]{1,0:T(8,128)(2,1)}, u32[]{:S(2)}) copy-start(bf16[896,1792]{1,0:T(8,128)(2,1)} %param.14) | copy-start | bytes 9633796
  7.2 67.2 %reduce-scatter.4.cloned.1.call-start = ((), (), s32[]{:S(2)}) async-start(), calls=%async_computation.1 | async-start | bytes 2064384 | tf_op jit(solution)/shard_map/reduce_scatter | solution.py:49
  69.6 160.9 %all-reduce.6.cloned.1.call-start = ((), (), s32[]{:S(2)}) async-start(), calls=%async_computation.2 | async-start | bytes 1572864 | tf_op jit(solution)/shard_map/psum | solution.py:65
  77.7 65.9 %copy-start.9 = (u32[32]{0:T(128)S(1)}, u32[32]{0:T(128)}, u32[]{:S(2)}) copy-start(u32[32]{0:T(128)} %constant.30) | copy-start | bytes 388
  79.6 77.5 %copy-start.4 = (bf16[12,1792]{1,0:T(8,128)(2,1)S(1)}, bf16[12,1792]{1,0:T(8,128)(2,1)}, u32[]{:S(2)}) copy-start(bf16[12,1792]{1,0:T(8,128)(2,1)} %param.10) | copy-start | bytes 129028
  79.6 77.5 %copy-start.8 = (f32[1792]{0:T(1024)S(1)}, f32[1792]{0:T(1024)}, u32[]{:S(2)}) copy-start(f32[1792]{0:T(1024)} %param.15) | copy-start | bytes 21508
  132.6 13.1 %collective-permute-start.2 = (f32[16,1792]{1,0:T(8,128)S(1)}, f32[16,1792]{1,0:T(8,128)S(1)}, u32[]{:S(2)}, u32[]{:S(2)}) collective-permute-start(f32[16,1792]{1,0:T(8,128)S(1)} %fusion), channel_id=1, source_target_pairs={{0,3},{1,4},{2,5},{3,6},{4,7},{5,8},{6,9},{7,10},{8,11},{9,12},{10... | collective-permute-start | bytes 344072
  133.9 11.8 %collective-permute-start.1 = (f32[16,1792]{1,0:T(8,128)S(1)}, f32[16,1792]{1,0:T(8,128)}, u32[]{:S(2)}, u32[]{:S(2)}) collective-permute-start(f32[16,1792]{1,0:T(8,128)S(1)} %fusion), channel_id=1, source_target_pairs={{0,2},{1,3},{2,4},{3,5},{4,6},{5,7},{6,8},{7,9},{8,10},{9,11},{10,... | collective-permute-start | bytes 344072
  138.4 7.3 %collective-permute-start = (f32[16,1792]{1,0:T(8,128)S(1)}, f32[16,1792]{1,0:T(8,128)}, u32[]{:S(2)}, u32[]{:S(2)}) collective-permute-start(f32[16,1792]{1,0:T(8,128)S(1)} %fusion), channel_id=1, source_target_pairs={{0,1},{1,2},{2,3},{3,4},{4,5},{5,6},{6,7},{7,8},{8,9},{9,10},{10,1... | collective-permute-start | bytes 344072
  141.2 4.4 %collective-permute-start.3 = (f32[12,1792]{1,0:T(8,128)}, f32[12,1792]{1,0:T(8,128)}, u32[]{:S(2)}, u32[]{:S(2)}) collective-permute-start(f32[12,1792]{1,0:T(8,128)} %slice.10), channel_id=1, source_target_pairs={{0,4},{1,5},{2,6},{3,7},{4,8},{5,9},{6,10},{7,11},{8,12},{9,13},{1... | collective-permute-start | bytes 258056
  158.1 57.1 %copy-start.5 = (bf16[12,1792]{1,0:T(8,128)(2,1)}, bf16[12,1792]{1,0:T(8,128)(2,1)S(1)}, u32[]{:S(2)}) copy-start(bf16[12,1792]{1,0:T(8,128)(2,1)S(1)} %fusion.23) | copy-start | bytes 129028
  207.9 22.6 %copy-start.6 = (f32[1024]{0:T(1024)S(1)}, f32[1024]{0:T(1024)}, u32[]{:S(2)}) copy-start(f32[1024]{0:T(1024)} %param.17) | copy-start | bytes 12292
  215.3 141.7 %copy-start.7 = (f32[1792]{0:T(1024)S(1)}, f32[1792]{0:T(1024)}, u32[]{:S(2)}) copy-start(f32[1792]{0:T(1024)} %param.19) | copy-start | bytes 21508
  215.3 141.7 %all-reduce.8.cloned.1.call-start = ((), (), s32[]{:S(2)}) async-start(), calls=%async_computation.3 | async-start | bytes 2752512 | tf_op jit(solution)/shard_map/psum | solution.py:70
  240.4 146.2 %all-reduce.10.cloned.1.call-start = ((), (), s32[]{:S(2)}) async-start(), calls=%async_computation.4 | async-start | bytes 786432 | tf_op jit(solution)/shard_map/psum | solution.py:80
  369.0 2.5 copy-start.1
  369.0 2.5 copy-start.3
  386.6 2.2 copy-start.2
Sparse Core Ops, SparseCore 0:
  69.7 4.6 reduce-scatter.3
  215.4 15.0 all-reduce.5
  240.5 116.4 all-reduce.7
  369.1 17.4 all-reduce.9
where the time goes:
time: 403 us; the launch traced here: 402 us
  blocking collectives  158 us (39%)
  waiting for transfers between devices  142 us (35%)
  matrix products  53.5 us (13%)
  between operations  14.5 us (4%)
  local copies, waits for them, and re-layouts  13.4 us (3%)
  starting transfers between devices  10.9 us (3%)
  other arithmetic  9.95 us (2%)
    psum x1, waiting for transfers between devices, body(): recon = lax.psum(partial_rec, ('lat', 'grp'))  116 us
    unnamed x1, blocking collectives  52.9 us
    all_gather x1, blocking collectives, body(): lax.all_gather(normed, ('lat', 'grp'), axis=0, tiled=True)  50 us
    all_gather x1, blocking collectives, body(): relayed = lax.all_gather(stream_out, ('lat', 'grp'), axis=0, tiled=True)  47.7 us
    psum x1, waiting for transfers between devices, body(): preact = lax.psum(encoded, 'row') + enc_bias  15 us
    unnamed x25, local copies, waits for them, and re-layouts  13.4 us
    dot_general x1, matrix products, body(): jnp.dot(residual_grad, dec_weight.T, precision=highest, preferred_element...  12 us
    unnamed x4, starting transfers between devices  10.4 us
  transfers between devices with their start and end apart: 8, of which 5 were waited for; matrix products, arithmetic and copies ran while one was open for 3% of the time, Pallas kernels for 0%

commit v1 on v0

v1 whole, which is shorter than its diff:
```python
import functools
import math

import jax
import jax.numpy as jnp
from jax import lax
from jax.experimental import pallas as pl
from jax.experimental.pallas import tpu as pltpu
from jax.sharding import PartitionSpec as P

epsilon = 1e-06
sparsity = 0.2
sharpness = 4.0
PAD = 16
f32 = jnp.float32
bf16 = jnp.bfloat16
MESH = pl.DeviceIdType.MESH


def each(n, f):
    if n > 0:
        lax.fori_loop(0, n, lambda i, c: (f(i), c)[1], 0)


def column_tiles(width, f, tile=256):
    whole = width // tile
    each(whole, lambda i: f(pl.ds(pl.multiple_of(i * tile, tile), tile)))
    if width % tile:
        f(pl.ds(whole * tile, width % tile))


def kernel(
    shape,
    stream_ref, pre_ref, post_ref, encb_ref, decb_ref,
    gate_hbm, up_hbm, down_hbm, enc_hbm, dec_hbm,
    out_ref, inputs_ref, lat_ref, resid_ref, pgrad_ref, gencb_ref, gdecb_ref,
    wg, wu, wd, wenc, wdec, enc16, dec16,
    xs, xg, gbuf, ubuf, sbuf, hidden, squares,
    part1, land1, mid1, far1, tbuf, ys,
    pbuf, preact, part2, land2, mid2, far2, rs, bbuf,
    wsem,
    ag_send, ag_recv, rs_send, rs_recv, rz_send, rz_recv, row_send, row_recv,
):
    rows, zs, qs, grps, real, width, tokens = shape
    n = zs * qs
    total = n * PAD
    row = lax.axis_index("row")
    me = lax.axis_index("lat") * grps + lax.axis_index("grp")
    z = me // qs
    q = lax.rem(me, qs)

    def at(shard):
        return {"lat": shard // grps, "grp": lax.rem(shard, grps)}

    def zpeer(d):
        return lax.rem(z + d, zs)

    def qpeer(d):
        return lax.rem(q + d, qs)

    def send(src, dst, s, r, dev):
        return pltpu.make_async_remote_copy(
            src_ref=src, dst_ref=dst, send_sem=s, recv_sem=r, device_id=dev, device_id_type=MESH
        )

    loads = [
        pltpu.make_async_copy(a, b, wsem.at[i])
        for i, (a, b) in enumerate(
            [(gate_hbm, wg), (up_hbm, wu), (down_hbm, wd), (enc_hbm, wenc), (dec_hbm, wdec)]
        )
    ]
    for load in loads:
        load.start()

    barrier = pltpu.get_barrier_semaphore()

    def hail(dev):
        pl.semaphore_signal(barrier, inc=1, device_id=dev, device_id_type=MESH)

    each(zs - 1, lambda i: hail(at(zpeer(i + 1) * qs + q)))
    each(qs - 1, lambda i: hail(at(z * qs + qpeer(i + 1))))
    each(rows - 1, lambda i: hail({"row": lax.rem(row + i + 1, rows)}))
    pl.semaphore_wait(barrier, zs - 1 + qs - 1 + rows - 1)

    def gather_copy(k, buf, shard, dev, slot):
        return send(buf.at[shard], buf.at[shard], ag_send.at[k, slot], ag_recv.at[k, shard], dev)

    def to_plane(k, buf, dz, shard, start):
        def one(i):
            c = gather_copy(k, buf, shard, at(z * qs + qpeer(i + 1)), dz * qs + i + 1)
            c.start() if start else c.wait_send()

        each(qs - 1, one)

    def gather_start(k, buf):
        each(
            zs - 1,
            lambda i: gather_copy(k, buf, me, at(zpeer(i + 1) * qs + q), (i + 1) * qs).start(),
        )
        to_plane(k, buf, 0, me, True)

    def gather_pass(k, buf):
        def one(i):
            shard = zpeer(i + 1) * qs + q
            gather_copy(k, buf, shard, at(shard), 0).wait_recv()
            to_plane(k, buf, i + 1, shard, True)

        each(zs - 1, one)

    def gather_end(k, buf):
        def one(dz):
            def two(i):
                shard = zpeer(dz) * qs + qpeer(i + 1)
                gather_copy(k, buf, shard, at(z * qs + qpeer(i + 1)), 0).wait_recv()

            each(qs - 1, two)

        each(zs, one)

        def sent(dz):
            to_plane(k, buf, dz, zpeer(dz) * qs + q, False)

        each(zs, sent)
        each(
            zs - 1,
            lambda i: gather_copy(k, buf, me, at(zpeer(i + 1) * qs + q), (i + 1) * qs).wait_send(),
        )

    def plane_out(k, part, land, zz, dq):
        to = qpeer(dq)
        return send(
            part.at[zz * qs + to], land.at[q, zz],
            rs_send.at[k, zz * qs + dq], rs_recv.at[k, zz * qs + q], at(z * qs + to),
        )

    def plane_in(k, part, land, zz, dq):
        of = qpeer(dq)
        return send(
            part.at[zz * qs + of], land.at[of, zz],
            rs_send.at[k, zz * qs + dq], rs_recv.at[k, zz * qs + of], at(z * qs + of),
        )

    def line(k, mid, far, dz):
        to = zpeer(dz)
        return send(mid.at[to], far.at[z], rz_send.at[k, to], rz_recv.at[k, z], at(to * qs + q))

    def line_in(k, mid, far, dz):
        of = zpeer(dz)
        return send(mid.at[of], far.at[of], rz_send.at[k, of], rz_recv.at[k, of], at(of * qs + q))

    def scatter_start(k, part, land):
        def one(dz):
            zz = zpeer(dz + 1)
            each(qs - 1, lambda i: plane_out(k, part, land, zz, i + 1).start())

        each(zs, one)

    def scatter_sum(k, part, land, mid, far):
        def plane_sum(zz):
            each(qs - 1, lambda i: plane_in(k, part, land, zz, i + 1).wait_recv())
            acc = part[zz * qs + q].astype(f32)
            for i in range(1, qs):
                acc = acc + land[qpeer(i), zz].astype(f32)
            return acc

        def one(i):
            zz = zpeer(i + 1)
            mid[zz] = plane_sum(zz).astype(bf16)
            line(k, mid, far, i + 1).start()

        each(zs - 1, one)
        acc = plane_sum(z)
        for dz in range(1, zs):
            line_in(k, mid, far, dz).wait_recv()
            acc = acc + far[zpeer(dz)].astype(f32)
        return acc

    def scatter_end(k, part, land, mid, far):
        def one(dz):
            each(qs - 1, lambda i: plane_out(k, part, land, zpeer(dz), i + 1).wait_send())

        each(zs, one)
        each(zs - 1, lambda i: line(k, mid, far, i + 1).wait_send())

    def row_out(k, buf, d):
        return send(
            buf.at[row], buf.at[row], row_send.at[k, d], row_recv.at[k, row],
            {"row": lax.rem(row + d, rows)},
        )

    def row_start(k, buf):
        each(rows - 1, lambda i: row_out(k, buf, i + 1).start())

    def row_wait(k, buf):
        def one(i):
            of = lax.rem(row + i + 1, rows)
            send(
                buf.at[of], buf.at[of], row_send.at[k, 0], row_recv.at[k, of], {"row": of}
            ).wait_recv()
            row_out(k, buf, i + 1).wait_send()

        each(rows - 1, one)

    def row_sum(buf, *index):
        acc = buf[(0, *index)].astype(f32)
        for i in range(1, rows):
            acc = acc + buf[(i, *index)].astype(f32)
        return acc

    def block(i):
        return pl.ds(pl.multiple_of(i * PAD, PAD), PAD)

    def cast(src, dst):
        tall = src.shape[0]
        chunk = 16

        def one(i):
            r = pl.ds(pl.multiple_of(i * chunk, chunk), chunk)
            dst[r, :] = src[r, :].astype(bf16)

        each(tall // chunk, one)

    xs[me] = stream_ref[...]
    gather_start(0, xs)
    gather_pass(0, xs)
    gather_end(0, xs)

    def norm_rows(i):
        x = xs[i].astype(f32)
        xg[block(i), :] = (x * pre_ref[...]).astype(bf16)
        sbuf[row, block(i), :] = jnp.broadcast_to(
            jnp.sum(x * x, axis=1, keepdims=True), (PAD, 128)
        )

    each(n, norm_rows)
    row_start(0, sbuf)

    def project(buf, w):
        def one(c):
            buf[row, :, c] = jnp.dot(xg[...], w[:, c], preferred_element_type=f32).astype(bf16)

        column_tiles(w.shape[1], one)

    loads[0].wait()
    project(gbuf, wg)
    row_start(1, gbuf)
    loads[1].wait()
    project(ubuf, wu)
    row_start(2, ubuf)
    loads[3].wait()
    row_wait(0, sbuf)
    row_wait(1, gbuf)
    row_wait(2, ubuf)

    def activate(i):
        r = lax.rsqrt(row_sum(sbuf, block(i))[:, :1] / width + epsilon)
        g = row_sum(gbuf, block(i)) * r
        u = row_sum(ubuf, block(i)) * r
        hidden[block(i), :] = (jax.nn.gelu(g, approximate=True) * u).astype(bf16)

    each(n, activate)
    loads[2].wait()

    def down(c):
        v = jnp.dot(hidden[...], wd[:, c], preferred_element_type=f32)
        part1[:, :, c] = v.astype(bf16).reshape(n, PAD, v.shape[1])

    column_tiles(wd.shape[1], down)
    scatter_start(0, part1, land1)
    cast(wenc, enc16)
    output = scatter_sum(0, part1, land1, mid1, far1)
    tbuf[row] = jnp.broadcast_to(jnp.sum(output * output, axis=1, keepdims=True), (PAD, 128))
    row_start(3, tbuf)
    row_wait(3, tbuf)
    scale_out = lax.rsqrt(row_sum(tbuf)[:, :1] / width + epsilon)
    mine = stream_ref[...].astype(f32) + output * scale_out * post_ref[...]
    stream_out = mine.astype(bf16)
    out_ref[...] = stream_out
    ys[me] = stream_out
    gather_start(1, ys)
    scatter_end(0, part1, land1, mid1, far1)
    loads[4].wait()
    gather_pass(1, ys)
    cast(wdec, dec16)
    gather_end(1, ys)
    inputs_ref[...] = ys[...].reshape(total, ys.shape[2])

    def encode(c):
        pbuf[row, :, c] = jnp.dot(
            ys[...].reshape(total, ys.shape[2]), enc16[:, c], preferred_element_type=f32
        ).astype(bf16)

    column_tiles(enc16.shape[1], encode)
    row_start(4, pbuf)
    row_wait(4, pbuf)

    def softplus(i):
        p = sharpness * (row_sum(pbuf, block(i)) + encb_ref[...])
        e = jnp.exp(-jnp.abs(p))
        lat_ref[block(i), :] = (
            (jnp.maximum(p, 0.0) + jnp.log1p(e)) * (1.0 / sharpness)
        ).astype(bf16)
        preact[block(i), :] = jnp.where(p >= 0, 1.0, e) / (1.0 + e)

    each(n, softplus)

    def decode(c):
        v = jnp.dot(lat_ref[...], dec16[:, c], preferred_element_type=f32)
        part2[:, :, c] = v.astype(bf16).reshape(n, PAD, v.shape[1])

    column_tiles(dec16.shape[1], decode)
    scatter_start(1, part2, land2)
    recon = scatter_sum(1, part2, land2, mid2, far2)
    scale = 1.0 / math.sqrt(tokens)
    keep = lax.broadcasted_iota(jnp.int32, (PAD, 1), 0) < real
    resid = jnp.where(keep, (recon + decb_ref[...] - ys[me].astype(f32)) * scale, 0.0)
    rs[me] = resid.astype(bf16)
    gather_start(2, rs)
    scatter_end(1, part2, land2, mid2, far2)
    gather_pass(2, rs)
    gather_end(2, rs)
    resid_ref[...] = rs[...].reshape(total, rs.shape[2])

    def back(c):
        bbuf[row, :, c] = lax.dot_general(
            rs[...].reshape(total, rs.shape[2]), dec16[c, :],
            (((1,), (1,)), ((), ())), preferred_element_type=f32,
        ).astype(bf16)

    column_tiles(dec16.shape[0], back)
    row_start(5, bbuf)

    gdecb_ref[...] = jnp.zeros_like(gdecb_ref)

    def dec_bias(i):
        gdecb_ref[...] += jnp.sum(rs[i].astype(f32), axis=0, keepdims=True)

    each(n, dec_bias)
    row_wait(5, bbuf)
    gencb_ref[...] = jnp.zeros_like(gencb_ref)

    def finish(i):
        g = (row_sum(bbuf, block(i)) + sparsity * scale) * preact[block(i), :]
        pgrad_ref[block(i), :] = g.astype(bf16)
        gencb_ref[...] += jnp.sum(jnp.where(keep, g, 0.0), axis=0, keepdims=True)

    each(n, finish)


def body(
    split, sizes,
    stream_in, pre_gain, gate_weight, up_weight, down_weight, post_gain,
    enc_weight, enc_bias, dec_weight, dec_bias,
):
    rows, zs, qs, grps = sizes
    n = zs * qs
    real, d = stream_in.shape
    hid = gate_weight.shape[1]
    lat = enc_weight.shape[1]
    total = n * PAD
    shape = (rows, zs, qs, grps, real, d * rows, real * n)
    vmem = pltpu.VMEM
    scratch = [
        vmem((d, hid), bf16), vmem((d, hid), bf16), vmem((hid, d), bf16),
        vmem((d, lat), f32), vmem((lat, d), f32), vmem((d, lat), bf16), vmem((lat, d), bf16),
        vmem((n, PAD, d), bf16), vmem((total, d), bf16),
        vmem((rows, total, hid), bf16), vmem((rows, total, hid), bf16),
        vmem((rows, total, 128), f32), vmem((total, hid), bf16), vmem((8, 128), f32),
        vmem((n, PAD, d), bf16), vmem((qs, zs, PAD, d), bf16),
        vmem((zs, PAD, d), bf16), vmem((zs, PAD, d), bf16),
        vmem((rows, PAD, 128), f32), vmem((n, PAD, d), bf16),
        vmem((rows, total, lat), bf16), vmem((total, lat), f32),
        vmem((n, PAD, d), bf16), vmem((qs, zs, PAD, d), bf16),
        vmem((zs, PAD, d), bf16), vmem((zs, PAD, d), bf16),
        vmem((n, PAD, d), bf16), vmem((rows, total, lat), bf16),
        pltpu.SemaphoreType.DMA((5,)),
        pltpu.SemaphoreType.DMA((3, n)), pltpu.SemaphoreType.DMA((3, n)),
        pltpu.SemaphoreType.DMA((2, n)), pltpu.SemaphoreType.DMA((2, n)),
        pltpu.SemaphoreType.DMA((2, zs)), pltpu.SemaphoreType.DMA((2, zs)),
        pltpu.SemaphoreType.DMA((6, rows)), pltpu.SemaphoreType.DMA((6, rows)),
    ]
    here = pl.BlockSpec(memory_space=pltpu.VMEM)
    there = pl.BlockSpec(memory_space=pl.ANY)
    sds = jax.ShapeDtypeStruct
    padded = jnp.pad(stream_in, ((0, PAD - real), (0, 0)))
    out, inputs, latents, resid, pgrad, gencb, gdecb = pl.pallas_call(
        functools.partial(kernel, shape),
        out_shape=(
            sds((PAD, d), bf16), sds((total, d), bf16), sds((total, lat), bf16),
            sds((total, d), bf16), sds((total, lat), bf16), sds((1, lat), f32), sds((1, d), f32),
        ),
        in_specs=[here] * 5 + [there] * 5,
        out_specs=[here] * 7,
        scratch_shapes=scratch,
        compiler_params=pltpu.CompilerParams(
            collective_id=0, has_side_effects=True, vmem_limit_bytes=60 * 1024 * 1024
        ),
    )(
        padded, pre_gain[None], post_gain[None], enc_bias[None], dec_bias[None],
        gate_weight, up_weight, down_weight, enc_weight, dec_weight,
    )
    grad_dec = jnp.dot(latents.T, resid, preferred_element_type=f32)
    grad_enc = jnp.dot(inputs.T, pgrad, preferred_element_type=f32)
    return (out[:real], grad_enc, gencb[0], grad_dec, gdecb[0])


def solution(mesh):
    rows, lats, grps = (mesh.shape[a] for a in ("row", "lat", "grp"))
    inner = max(i for i in range(1, lats + 1) if lats % i == 0 and i * i <= lats)
    sizes = (rows, lats // inner, inner * grps, grps)
    both = ("lat", "grp")
    placed = (
        P(both, "row"), P("row"), P("row", both), P("row", both), P(both, "row"),
        P("row"), P("row", both), P(both), P(both, "row"), P("row"),
    )
    return jax.shard_map(
        functools.partial(body, None, sizes),
        mesh=mesh,
        in_specs=placed,
        out_specs=(P(both, "row"), P("row", both), P(both), P(both, "row"), P("row")),
        check_vma=False,
    )
```

time: 403 us -> 121 us (0.30)
  blocking collectives: 158 us -> 0 us
  waiting for transfers between devices: 142 us -> 0 us
  Pallas kernels: 0 us -> 102 us
  matrix products: 53.5 us -> 9.86 us
  between operations: 14.5 us -> 0.67 us
  starting transfers between devices: 10.9 us -> 0 us
  other arithmetic: 9.95 us -> 0.62 us
  local copies, waits for them, and re-layouts: 13.4 us -> 6.57 us
    psum x3 -> x0, waiting for transfers between devices: 136 us -> none  [the longest x1 116 us: body(): recon = lax.psum(partial_rec, ('lat', 'grp'))]
    pallas_call x0 -> x1, Pallas kernels: none -> 102 us  [body(): pl.pallas_call(functools.partial(kernel, shape), out_shape=(sds((PAD, d),...]
    all_gather x3 -> x0, blocking collectives: 99.8 us -> none  [the longest x1 50 us: body(): lax.all_gather(normed, ('lat', 'grp'), axis=0, tiled=True)]
    unnamed x1 -> x0, blocking collectives: 52.9 us -> none
    dot_general x7 -> x2, matrix products: 53.5 us -> 9.86 us  [the longest x1 5.67 us: body(): grad_dec = jnp.dot(latents.T, resid, preferred_element_type=f32)]
    unnamed x25 -> x12, local copies, waits for them, and re-layouts: 13.4 us -> 1.24 us
    unnamed x4 -> x0, starting transfers between devices: 10.4 us -> none
    reduce_sum x4 -> x0, other arithmetic: 6.81 us -> none  [the longest x1 2.49 us: body(): grad_dec_bias = jnp.sum(residual_grad, axis=0)]
  transfers between devices with their start and end apart: 8 -> 0, of which waited for: 5 -> 0; matrix products, arithmetic and copies ran while one was open for 3% -> 0% of each run, Pallas kernels for 0% -> 0%
where the time goes in v1:
time: 121 us; the launch traced here: 120 us
  Pallas kernels  102 us (84%)
  matrix products  9.86 us (8%)
  local copies, waits for them, and re-layouts  6.57 us (5%)
    pallas_call x1, Pallas kernels, body(): pl.pallas_call(functools.partial(kernel, shape), out_shape=(sds((PAD, d),...  102 us
    dot_general x1, matrix products, body(): grad_dec = jnp.dot(latents.T, resid, preferred_element_type=f32)  5.67 us
    dot_general x1, matrix products, body(): grad_enc = jnp.dot(inputs.T, pgrad, preferred_element_type=f32)  4.19 us

profile of v1, /device:TPU:0, one launch (start us, length us, event | category | flops | bytes accessed | tf_op | source)
XLA Modules:
  0.0 120.2 jit_solution(10080984075956423671)
XLA Ops:
  0.6 1.5 %pad.4.stream_ref = bf16[16,1792]{1,0:T(8,128)(2,1)} pad(bf16[12,1792]{1,0:T(8,128)(2,1)} %param.10, bf16[]{:T(256)} %constant.2.clone.1), padding=0_4x0_0 | pad | bytes 100354 | tf_op jit(solution)/shard_map/jit(_pad)/pad | solution.py:385
  2.1 1.3 %broadcast_in_dim.12.pre_ref = f32[1,1792]{1,0:T(1,128)} reshape(f32[1792]{0:T(1024)} %param.11) | data formatting | bytes 14336 | tf_op jit(solution)/shard_map/broadcast_in_dim | solution.py:399
  3.4 1.3 %broadcast_in_dim.13.post_ref = f32[1,1792]{1,0:T(1,128)} reshape(f32[1792]{0:T(1024)} %param.15) | data formatting | bytes 14336 | tf_op jit(solution)/shard_map/broadcast_in_dim | solution.py:399
  4.7 1.3 %broadcast_in_dim.15.decb_ref = f32[1,1792]{1,0:T(1,128)} reshape(f32[1792]{0:T(1024)} %param.19) | data formatting | bytes 14336 | tf_op jit(solution)/shard_map/broadcast_in_dim | solution.py:399
  6.0 102.5 %shard_map.137 = (bf16[16,1792]{1,0:T(8,128)(2,1)}, bf16[256,1792]{1,0:T(8,128)(2,1)}, bf16[256,1024]{1,0:T(8,128)(2,1)}, bf16[256,1792]{1,0:T(8,128)(2,1)}, bf1...) custom-call(bf16[16,1792]{1,0:T(8,128)(2,1)} %pad.4.stream_ref, f32[1,1792]{1,0:T(1,128)} %broadcast_in_dim.12.pre_ref, ...), custom_call_target="tpu_custom_call" | custom-call | tf_op jit(solution)/shard_map/pallas_call | solution.py:386
  108.5 0.0 copy-start
  108.5 0.0 copy-start.1
  108.5 5.7 %fusion.1 = f32[1024,1792]{1,0:T(8,128)} fusion(bf16[256,1024]{1,0:T(8,128)(2,1)} %get-tuple-element.16, bf16[256,1792]{1,0:T(8,128)(2,1)} %get-tuple-element.17), kind=kOutput, calls=%fused_computation.1 | convolution fusion | flops 939524096 | bytes 8781824 | tf_op jit(solution)/shard_map/dot_general | solution.py:402
  114.2 0.0 copy-start.3
  114.2 0.0 copy-start.2
  114.2 0.0 copy-start.4
  114.2 0.0 copy-done
  114.2 0.0 copy-done.1
  114.2 4.2 %fusion = f32[1792,1024]{1,0:T(8,128)} fusion(bf16[256,1792]{1,0:T(8,128)(2,1)S(1)} %copy-done, bf16[256,1024]{1,0:T(8,128)(2,1)S(1)} %copy-done.1), kind=kOutput, calls=%fused_computation | convolution fusion | flops 939524096 | bytes 8781824 | tf_op jit(solution)/shard_map/dot_general | solution.py:403
  118.4 0.0 copy-done.3
  118.4 0.6 reduce
  119.0 0.0 copy-done.2
  119.0 0.6 copy.17
  119.6 0.0 copy-done.4
  119.6 0.6 copy.18
Async XLA Ops:
  108.5 5.7 %copy-start = (bf16[256,1792]{1,0:T(8,128)(2,1)S(1)}, bf16[256,1792]{1,0:T(8,128)(2,1)}, u32[]{:S(2)}) copy-start(bf16[256,1792]{1,0:T(8,128)(2,1)} %get-tuple-element.13) | copy-start | bytes 2752516
  108.5 5.7 %copy-start.1 = (bf16[256,1024]{1,0:T(8,128)(2,1)S(1)}, bf16[256,1024]{1,0:T(8,128)(2,1)}, u32[]{:S(2)}) copy-start(bf16[256,1024]{1,0:T(8,128)(2,1)} %get-tuple-element.14) | copy-start | bytes 1572868
  114.2 4.2 %copy-start.3 = (f32[1,1792]{1,0:T(1,128)S(1)}, f32[1,1792]{1,0:T(1,128)}, u32[]{:S(2)}) copy-start(f32[1,1792]{1,0:T(1,128)} %get-tuple-element.18) | copy-start | bytes 21508
  114.2 4.8 %copy-start.2 = (bf16[16,1792]{1,0:T(8,128)(2,1)S(1)}, bf16[16,1792]{1,0:T(8,128)(2,1)}, u32[]{:S(2)}) copy-start(bf16[16,1792]{1,0:T(8,128)(2,1)} %get-tuple-element.12) | copy-start | bytes 172036
  114.2 5.5 %copy-start.4 = (f32[1,1024]{1,0:T(1,128)S(1)}, f32[1,1024]{1,0:T(1,128)}, u32[]{:S(2)}) copy-start(f32[1,1024]{1,0:T(1,128)} %get-tuple-element.15) | copy-start | bytes 12292

commit v2 on v1

--- a/solution.py
+++ b/solution.py
@@ -31,13 +31,14 @@
 
 def kernel(
     shape,
-    stream_ref, pre_ref, post_ref, encb_ref, decb_ref,
+    stream_hbm, pre_hbm, post_hbm, encb_hbm, decb_hbm,
     gate_hbm, up_hbm, down_hbm, enc_hbm, dec_hbm,
     out_ref, inputs_ref, lat_ref, resid_ref, pgrad_ref, gencb_ref, gdecb_ref,
     wg, wu, wd, wenc, wdec, enc16, dec16,
     xs, xg, gbuf, ubuf, sbuf, hidden, squares,
     part1, land1, mid1, far1, tbuf, ys,
     pbuf, preact, part2, land2, mid2, far2, rs, bbuf,
+    pre_ref, post_ref, encb_ref, decb_ref,
     wsem,
     ag_send, ag_recv, rs_send, rs_recv, rz_send, rz_recv, row_send, row_recv,
 ):
@@ -66,10 +67,14 @@
     loads = [
         pltpu.make_async_copy(a, b, wsem.at[i])
         for i, (a, b) in enumerate(
-            [(gate_hbm, wg), (up_hbm, wu), (down_hbm, wd), (enc_hbm, wenc), (dec_hbm, wdec)]
+            [
+                (gate_hbm, wg), (up_hbm, wu), (down_hbm, wd), (enc_hbm, wenc), (dec_hbm, wdec),
+                (pre_hbm, pre_ref), (post_hbm, post_ref), (encb_hbm, encb_ref),
+                (decb_hbm, decb_ref), (stream_hbm, xs.at[me]),
+            ]
         )
     ]
-    for load in loads:
+    for load in loads[5:] + loads[:5]:
         load.start()
 
     barrier = pltpu.get_barrier_semaphore()
@@ -107,11 +112,14 @@
 
         each(zs - 1, one)
 
-    def gather_end(k, buf):
+    def gather_end(k, buf, done):
         def one(dz):
+            done(zpeer(dz) * qs + q)
+
             def two(i):
                 shard = zpeer(dz) * qs + qpeer(i + 1)
                 gather_copy(k, buf, shard, at(z * qs + qpeer(i + 1)), 0).wait_recv()
+                done(shard)
 
             each(qs - 1, two)
 
@@ -210,6 +218,18 @@
     def block(i):
         return pl.ds(pl.multiple_of(i * PAD, PAD), PAD)
 
+    def fill(v):
+        return jnp.concatenate([v, jnp.zeros((PAD - real, v.shape[1]), v.dtype)], axis=0)
+
+    def line_of(ref):
+        return ref[...].reshape(1, ref.shape[0])
+
+    def widen(buf, dst):
+        def one(i):
+            dst[block(i), :] = fill(buf[i].astype(f32)).astype(bf16)
+
+        return one
+
     def cast(src, dst):
         tall = src.shape[0]
         chunk = 16
@@ -220,19 +240,20 @@
 
         each(tall // chunk, one)
 
-    xs[me] = stream_ref[...]
+    loads[9].wait()
     gather_start(0, xs)
+    for load in loads[5:9]:
+        load.wait()
     gather_pass(0, xs)
-    gather_end(0, xs)
 
     def norm_rows(i):
-        x = xs[i].astype(f32)
-        xg[block(i), :] = (x * pre_ref[...]).astype(bf16)
+        x = fill(xs[i].astype(f32))
+        xg[block(i), :] = (x * line_of(pre_ref)).astype(bf16)
         sbuf[row, block(i), :] = jnp.broadcast_to(
             jnp.sum(x * x, axis=1, keepdims=True), (PAD, 128)
         )
 
-    each(n, norm_rows)
+    gather_end(0, xs, norm_rows)
     row_start(0, sbuf)
 
     def project(buf, w):
@@ -263,17 +284,17 @@
 
     def down(c):
         v = jnp.dot(hidden[...], wd[:, c], preferred_element_type=f32)
-        part1[:, :, c] = v.astype(bf16).reshape(n, PAD, v.shape[1])
+        part1[:, :, c] = v.reshape(n, PAD, v.shape[1])[:, :real, :].astype(bf16)
 
     column_tiles(wd.shape[1], down)
     scatter_start(0, part1, land1)
     cast(wenc, enc16)
     output = scatter_sum(0, part1, land1, mid1, far1)
-    tbuf[row] = jnp.broadcast_to(jnp.sum(output * output, axis=1, keepdims=True), (PAD, 128))
+    tbuf[row] = jnp.broadcast_to(jnp.sum(output * output, axis=1, keepdims=True), (real, 128))
     row_start(3, tbuf)
     row_wait(3, tbuf)
     scale_out = lax.rsqrt(row_sum(tbuf)[:, :1] / width + epsilon)
-    mine = stream_ref[...].astype(f32) + output * scale_out * post_ref[...]
+    mine = xs[me].astype(f32) + output * scale_out * line_of(post_ref)
     stream_out = mine.astype(bf16)
     out_ref[...] = stream_out
     ys[me] = stream_out
@@ -282,12 +303,11 @@
     loads[4].wait()
     gather_pass(1, ys)
     cast(wdec, dec16)
-    gather_end(1, ys)
-    inputs_ref[...] = ys[...].reshape(total, ys.shape[2])
+    gather_end(1, ys, widen(ys, inputs_ref))
 
     def encode(c):
         pbuf[row, :, c] = jnp.dot(
-            ys[...].reshape(total, ys.shape[2]), enc16[:, c], preferred_element_type=f32
+            inputs_ref[...], enc16[:, c], preferred_element_type=f32
         ).astype(bf16)
 
     column_tiles(enc16.shape[1], encode)
@@ -295,7 +315,7 @@
     row_wait(4, pbuf)
 
     def softplus(i):
-        p = sharpness * (row_sum(pbuf, block(i)) + encb_ref[...])
+        p = sharpness * (row_sum(pbuf, block(i)) + line_of(encb_ref))
         e = jnp.exp(-jnp.abs(p))
         lat_ref[block(i), :] = (
             (jnp.maximum(p, 0.0) + jnp.log1p(e)) * (1.0 / sharpness)
@@ -306,24 +326,23 @@
 
     def decode(c):
         v = jnp.dot(lat_ref[...], dec16[:, c], preferred_element_type=f32)
-        part2[:, :, c] = v.astype(bf16).reshape(n, PAD, v.shape[1])
+        part2[:, :, c] = v.reshape(n, PAD, v.shape[1])[:, :real, :].astype(bf16)
 
     column_tiles(dec16.shape[1], decode)
     scatter_start(1, part2, land2)
     recon = scatter_sum(1, part2, land2, mid2, far2)
     scale = 1.0 / math.sqrt(tokens)
     keep = lax.broadcasted_iota(jnp.int32, (PAD, 1), 0) < real
-    resid = jnp.where(keep, (recon + decb_ref[...] - ys[me].astype(f32)) * scale, 0.0)
+    resid = (recon + line_of(decb_ref) - ys[me].astype(f32)) * scale
     rs[me] = resid.astype(bf16)
     gather_start(2, rs)
     scatter_end(1, part2, land2, mid2, far2)
     gather_pass(2, rs)
-    gather_end(2, rs)
-    resid_ref[...] = rs[...].reshape(total, rs.shape[2])
+    gather_end(2, rs, widen(rs, resid_ref))
 
     def back(c):
         bbuf[row, :, c] = lax.dot_general(
-            rs[...].reshape(total, rs.shape[2]), dec16[c, :],
+            resid_ref[...], dec16[c, :],
             (((1,), (1,)), ((), ())), preferred_element_type=f32,
         ).astype(bf16)
 
@@ -363,17 +382,18 @@
     scratch = [
         vmem((d, hid), bf16), vmem((d, hid), bf16), vmem((hid, d), bf16),
         vmem((d, lat), f32), vmem((lat, d), f32), vmem((d, lat), bf16), vmem((lat, d), bf16),
-        vmem((n, PAD, d), bf16), vmem((total, d), bf16),
+        vmem((n, real, d), bf16), vmem((total, d), bf16),
         vmem((rows, total, hid), bf16), vmem((rows, total, hid), bf16),
         vmem((rows, total, 128), f32), vmem((total, hid), bf16), vmem((8, 128), f32),
-        vmem((n, PAD, d), bf16), vmem((qs, zs, PAD, d), bf16),
-        vmem((zs, PAD, d), bf16), vmem((zs, PAD, d), bf16),
-        vmem((rows, PAD, 128), f32), vmem((n, PAD, d), bf16),
+        vmem((n, real, d), bf16), vmem((qs, zs, real, d), bf16),
+        vmem((zs, real, d), bf16), vmem((zs, real, d), bf16),
+        vmem((rows, real, 128), f32), vmem((n, real, d), bf16),
         vmem((rows, total, lat), bf16), vmem((total, lat), f32),
-        vmem((n, PAD, d), bf16), vmem((qs, zs, PAD, d), bf16),
-        vmem((zs, PAD, d), bf16), vmem((zs, PAD, d), bf16),
-        vmem((n, PAD, d), bf16), vmem((rows, total, lat), bf16),
-        pltpu.SemaphoreType.DMA((5,)),
+        vmem((n, real, d), bf16), vmem((qs, zs, real, d), bf16),
+        vmem((zs, real, d), bf16), vmem((zs, real, d), bf16),
+        vmem((n, real, d), bf16), vmem((rows, total, lat), bf16),
+        vmem((d,), f32), vmem((d,), f32), vmem((lat,), f32), vmem((d,), f32),
+        pltpu.SemaphoreType.DMA((10,)),
         pltpu.SemaphoreType.DMA((3, n)), pltpu.SemaphoreType.DMA((3, n)),
         pltpu.SemaphoreType.DMA((2, n)), pltpu.SemaphoreType.DMA((2, n)),
         pltpu.SemaphoreType.DMA((2, zs)), pltpu.SemaphoreType.DMA((2, zs)),
@@ -382,26 +402,25 @@
     here = pl.BlockSpec(memory_space=pltpu.VMEM)
     there = pl.BlockSpec(memory_space=pl.ANY)
     sds = jax.ShapeDtypeStruct
-    padded = jnp.pad(stream_in, ((0, PAD - real), (0, 0)))
     out, inputs, latents, resid, pgrad, gencb, gdecb = pl.pallas_call(
         functools.partial(kernel, shape),
         out_shape=(
-            sds((PAD, d), bf16), sds((total, d), bf16), sds((total, lat), bf16),
+            sds((real, d), bf16), sds((total, d), bf16), sds((total, lat), bf16),
             sds((total, d), bf16), sds((total, lat), bf16), sds((1, lat), f32), sds((1, d), f32),
         ),
-        in_specs=[here] * 5 + [there] * 5,
+        in_specs=[there] * 10,
         out_specs=[here] * 7,
         scratch_shapes=scratch,
         compiler_params=pltpu.CompilerParams(
             collective_id=0, has_side_effects=True, vmem_limit_bytes=60 * 1024 * 1024
         ),
     )(
-        padded, pre_gain[None], post_gain[None], enc_bias[None], dec_bias[None],
+        stream_in, pre_gain, post_gain, enc_bias, dec_bias,
         gate_weight, up_weight, down_weight, enc_weight, dec_weight,
     )
     grad_dec = jnp.dot(latents.T, resid, preferred_element_type=f32)
     grad_enc = jnp.dot(inputs.T, pgrad, preferred_element_type=f32)
-    return (out[:real], grad_enc, gencb[0], grad_dec, gdecb[0])
+    return (out, grad_enc, gencb[0], grad_dec, gdecb[0])
 
 
 def solution(mesh):

time: 121 us -> 113 us (0.934)
  local copies, waits for them, and re-layouts: 6.57 us -> 1.24 us
  Pallas kernels: 102 us -> 100 us
    broadcast_in_dim x3 -> x0, local copies, waits for them, and re-layouts: 3.88 us -> none  [the longest x1 1.29 us: body(): pre_gain[None]]
    pallas_call x1, Pallas kernels: 102 us -> 100 us  [body(): pl.pallas_call(functools.partial(kernel, shape), out_shape=(sds((real, d)...]
    pad x1 -> x0, local copies, waits for them, and re-layouts: 1.45 us -> none  [body(): padded = jnp.pad(stream_in, ((0, PAD - real), (0, 0)))]
where the time goes in v2:
time: 113 us
  Pallas kernels  100 us (88%)
  matrix products  9.86 us (9%)
  local copies, waits for them, and re-layouts  1.24 us (1%)
    pallas_call x1, Pallas kernels, body(): pl.pallas_call(functools.partial(kernel, shape), out_shape=(sds((real, d)...  100 us
    dot_general x1, matrix products, body(): grad_dec = jnp.dot(latents.T, resid, preferred_element_type=f32)  5.66 us
    dot_general x1, matrix products, body(): grad_enc = jnp.dot(inputs.T, pgrad, preferred_element_type=f32)  4.19 us

profile of v2, /device:TPU:0, one launch (start us, length us, event | category | flops | bytes accessed | tf_op | source)
XLA Modules:
  0.0 112.7 jit_solution(7931158876349016803)
XLA Ops:
  0.6 100.3 %shard_map.137 = (bf16[12,1792]{1,0:T(8,128)(2,1)}, bf16[256,1792]{1,0:T(8,128)(2,1)}, bf16[256,1024]{1,0:T(8,128)(2,1)}, bf16[256,1792]{1,0:T(8,128)(2,1)}, bf1...) custom-call(bf16[12,1792]{1,0:T(8,128)(2,1)} %stream_hbm.1, f32[1792]{0:T(1024)} %pre_hbm.1, ...), custom_call_target="tpu_custom_call" | custom-call | tf_op jit(solution)/shard_map/pallas_call | solution.py:405
  100.9 0.0 copy-start
  100.9 0.0 copy-start.1
  100.9 5.7 %fusion.1 = f32[1024,1792]{1,0:T(8,128)} fusion(bf16[256,1024]{1,0:T(8,128)(2,1)} %get-tuple-element.16, bf16[256,1792]{1,0:T(8,128)(2,1)} %get-tuple-element.17), kind=kOutput, calls=%fused_computation.1 | convolution fusion | flops 939524096 | bytes 8781824 | tf_op jit(solution)/shard_map/dot_general | solution.py:421
  106.6 0.0 copy-start.3
  106.6 0.0 copy-start.2
  106.6 0.0 copy-start.4
  106.6 0.0 copy-done
  106.6 0.0 copy-done.1
  106.6 4.2 %fusion = f32[1792,1024]{1,0:T(8,128)} fusion(bf16[256,1792]{1,0:T(8,128)(2,1)S(1)} %copy-done, bf16[256,1024]{1,0:T(8,128)(2,1)S(1)} %copy-done.1), kind=kOutput, calls=%fused_computation | convolution fusion | flops 939524096 | bytes 8781824 | tf_op jit(solution)/shard_map/dot_general | solution.py:422
  110.8 0.0 copy-done.3
  110.8 0.6 reduce
  111.4 0.0 copy-done.2
  111.4 0.6 copy.17
  112.1 0.0 copy-done.4
  112.1 0.6 copy.18
Async XLA Ops:
  100.9 5.7 %copy-start = (bf16[256,1792]{1,0:T(8,128)(2,1)S(1)}, bf16[256,1792]{1,0:T(8,128)(2,1)}, u32[]{:S(2)}) copy-start(bf16[256,1792]{1,0:T(8,128)(2,1)} %get-tuple-element.13) | copy-start | bytes 2752516
  100.9 5.7 %copy-start.1 = (bf16[256,1024]{1,0:T(8,128)(2,1)S(1)}, bf16[256,1024]{1,0:T(8,128)(2,1)}, u32[]{:S(2)}) copy-start(bf16[256,1024]{1,0:T(8,128)(2,1)} %get-tuple-element.14) | copy-start | bytes 1572868
  106.6 4.2 %copy-start.3 = (f32[1,1792]{1,0:T(1,128)S(1)}, f32[1,1792]{1,0:T(1,128)}, u32[]{:S(2)}) copy-start(f32[1,1792]{1,0:T(1,128)} %get-tuple-element.18) | copy-start | bytes 21508
  106.6 4.8 %copy-start.2 = (bf16[12,1792]{1,0:T(8,128)(2,1)S(1)}, bf16[12,1792]{1,0:T(8,128)(2,1)}, u32[]{:S(2)}) copy-start(bf16[12,1792]{1,0:T(8,128)(2,1)} %get-tuple-element.24) | copy-start | bytes 129028
  106.6 5.5 %copy-start.4 = (f32[1,1024]{1,0:T(1,128)S(1)}, f32[1,1024]{1,0:T(1,128)}, u32[]{:S(2)}) copy-start(f32[1,1024]{1,0:T(1,128)} %get-tuple-element.15) | copy-start | bytes 12292

commit v3 on v2

--- a/solution.py
+++ b/solution.py
@@ -199,6 +199,15 @@
     def row_start(k, buf):
         each(rows - 1, lambda i: row_out(k, buf, i + 1).start())
 
+    def row_piece(k, buf, c):
+        def one(i):
+            send(
+                buf.at[row, :, c], buf.at[row, :, c], row_send.at[k, i + 1],
+                row_recv.at[k, row], {"row": lax.rem(row + i + 1, rows)},
+            ).start()
+
+        each(rows - 1, one)
+
     def row_wait(k, buf):
         def one(i):
             of = lax.rem(row + i + 1, rows)
@@ -256,18 +265,17 @@
     gather_end(0, xs, norm_rows)
     row_start(0, sbuf)
 
-    def project(buf, w):
+    def project(k, buf, w):
         def one(c):
             buf[row, :, c] = jnp.dot(xg[...], w[:, c], preferred_element_type=f32).astype(bf16)
+            row_piece(k, buf, c)
 
         column_tiles(w.shape[1], one)
 
     loads[0].wait()
-    project(gbuf, wg)
-    row_start(1, gbuf)
+    project(1, gbuf, wg)
     loads[1].wait()
-    project(ubuf, wu)
-    row_start(2, ubuf)
+    project(2, ubuf, wu)
     loads[3].wait()
     row_wait(0, sbuf)
     row_wait(1, gbuf)
@@ -309,9 +317,9 @@
         pbuf[row, :, c] = jnp.dot(
             inputs_ref[...], enc16[:, c], preferred_element_type=f32
         ).astype(bf16)
+        row_piece(4, pbuf, c)
 
     column_tiles(enc16.shape[1], encode)
-    row_start(4, pbuf)
     row_wait(4, pbuf)
 
     def softplus(i):
@@ -345,9 +353,9 @@
             resid_ref[...], dec16[c, :],
             (((1,), (1,)), ((), ())), preferred_element_type=f32,
         ).astype(bf16)
+        row_piece(5, bbuf, c)
 
     column_tiles(dec16.shape[0], back)
-    row_start(5, bbuf)
 
     gdecb_ref[...] = jnp.zeros_like(gdecb_ref)
 
@@ -364,6 +372,32 @@
         gencb_ref[...] += jnp.sum(jnp.where(keep, g, 0.0), axis=0, keepdims=True)
 
     each(n, finish)
+
+
+def gradients(
+    steps, inputs_ref, pgrad_ref, lat_ref, resid_ref, gencb_in, gdecb_in, out_in,
+    genc_ref, gdec_ref, gencb_ref, gdecb_ref, out_ref,
+):
+    i = pl.program_id(0)
+    over_rows = (((0,), (0,)), ((), ()))
+
+    @pl.when(i == 0)
+    def _():
+        gencb_ref[...] = gencb_in[...].reshape(gencb_ref.shape)
+        gdecb_ref[...] = gdecb_in[...].reshape(gdecb_ref.shape)
+        out_ref[...] = out_in[...]
+
+    @pl.when(i < steps)
+    def _():
+        genc_ref[...] = lax.dot_general(
+            inputs_ref[...], pgrad_ref[...], over_rows, preferred_element_type=f32
+        )
+
+    @pl.when(i >= steps)
+    def _():
+        gdec_ref[...] = lax.dot_general(
+            lat_ref[...], resid_ref[...], over_rows, preferred_element_type=f32
+        )
 
 
 def body(
@@ -418,9 +452,34 @@
         stream_in, pre_gain, post_gain, enc_bias, dec_bias,
         gate_weight, up_weight, down_weight, enc_weight, dec_weight,
     )
-    grad_dec = jnp.dot(latents.T, resid, preferred_element_type=f32)
-    grad_enc = jnp.dot(inputs.T, pgrad, preferred_element_type=f32)
-    return (out, grad_enc, gencb[0], grad_dec, gdecb[0])
+    tall_enc = 256 if d % 256 == 0 else d
+    tall_dec = 256 if lat % 256 == 0 else lat
+    steps = d // tall_enc
+
+    def whole(*dims):
+        return pl.BlockSpec(dims, lambda i: (0,) * len(dims))
+
+    grad_enc, grad_dec, grad_encb, grad_decb, stream_out = pl.pallas_call(
+        functools.partial(gradients, steps),
+        grid=(steps + lat // tall_dec,),
+        out_shape=(
+            sds((d, lat), f32), sds((lat, d), f32), sds((lat,), f32), sds((d,), f32),
+            sds((real, d), bf16),
+        ),
+        in_specs=[
+            pl.BlockSpec((total, tall_enc), lambda i: (0, jnp.minimum(i, steps - 1))),
+            whole(total, lat),
+            pl.BlockSpec((total, tall_dec), lambda i: (0, jnp.maximum(i - steps, 0))),
+            whole(total, d), whole(1, lat), whole(1, d), whole(real, d),
+        ],
+        out_specs=(
+            pl.BlockSpec((tall_enc, lat), lambda i: (jnp.minimum(i, steps - 1), 0)),
+            pl.BlockSpec((tall_dec, d), lambda i: (jnp.maximum(i - steps, 0), 0)),
+            whole(lat), whole(d), whole(real, d),
+        ),
+        compiler_params=pltpu.CompilerParams(vmem_limit_bytes=32 * 1024 * 1024),
+    )(inputs, pgrad, latents, resid, gencb, gdecb, out)
+    return (stream_out, grad_enc, grad_encb, grad_dec, grad_decb)
 
 
 def solution(mesh):

time: 113 us -> 115 us (1.018)
  matrix products: 9.86 us -> 0 us
  Pallas kernels: 100 us -> 107 us
  local copies, waits for them, and re-layouts: 1.24 us -> 6.62 us
    dot_general x2 -> x0, matrix products: 9.86 us -> none  [the longest x1 5.66 us: body(): grad_dec = jnp.dot(latents.T, resid, preferred_element_type=f32)]
    pallas_call x0 -> x1, Pallas kernels: none -> 8.72 us  [body(): pl.pallas_call(functools.partial(gradients, steps), grid=(steps + lat //...]
    unnamed x12 -> x14, local copies, waits for them, and re-layouts: 1.24 us -> 6.62 us
    pallas_call x1, Pallas kernels: 100 us -> 98.7 us  [body(): pl.pallas_call(functools.partial(kernel, shape), out_shape=(sds((real, d)...]
where the time goes in v3:
time: 115 us
  Pallas kernels  107 us (93%)
  local copies, waits for them, and re-layouts  6.62 us (6%)
    pallas_call x1, Pallas kernels, body(): pl.pallas_call(functools.partial(kernel, shape), out_shape=(sds((real, d)...  98.7 us
    pallas_call x1, Pallas kernels, body(): pl.pallas_call(functools.partial(gradients, steps), grid=(steps + lat //...  8.72 us
    unnamed x14, local copies, waits for them, and re-layouts  6.62 us

profile of v3, /device:TPU:0, one launch (start us, length us, event | category | flops | bytes accessed | tf_op | source)
XLA Modules:
  0.0 114.7 jit_solution(2943476858680167358)
XLA Ops:
  0.6 98.7 %shard_map.137 = (bf16[12,1792]{1,0:T(8,128)(2,1)}, bf16[256,1792]{1,0:T(8,128)(2,1)}, bf16[256,1024]{1,0:T(8,128)(2,1)}, bf16[256,1792]{1,0:T(8,128)(2,1)}, bf1...) custom-call(bf16[12,1792]{1,0:T(8,128)(2,1)} %stream_hbm.1, f32[1792]{0:T(1024)} %pre_hbm.1, ...), custom_call_target="tpu_custom_call" | custom-call | tf_op jit(solution)/shard_map/pallas_call | solution.py:439
  99.3 0.0 copy-start
  99.3 1.2 %copy-done = bf16[256,1792]{1,0:T(8,128)(2,1)S(1)} copy-done((bf16[256,1792]{1,0:T(8,128)(2,1)S(1)}, bf16[256,1792]{1,0:T(8,128)(2,1)}, u32[]{:S(2)}) %copy-start) | copy-done | bytes 917528
  100.5 0.0 copy-start.1
  100.5 1.2 %copy-done.1 = bf16[256,1792]{1,0:T(8,128)(2,1)S(1)} copy-done((bf16[256,1792]{1,0:T(8,128)(2,1)S(1)}, bf16[256,1792]{1,0:T(8,128)(2,1)}, u32[]{:S(2)}) %copy-start.1) | copy-done | bytes 917528
  101.7 0.0 copy-start.2
  101.7 1.0 copy-done.2
  102.7 0.0 copy-start.3
  102.7 1.0 copy-done.3
  103.7 0.0 copy-start.4
  103.7 0.8 copy-done.4
  104.6 0.0 copy-start.5
  104.6 0.7 copy-done.5
  105.3 0.0 copy-start.6
  105.3 0.7 copy-done.6
  105.9 8.7 %shard_map.138 = (f32[1792,1024]{1,0:T(8,128)}, f32[1024,1792]{1,0:T(8,128)}, f32[1024]{0:T(1024)}, f32[1792]{0:T(1024)}, bf16[12,1792]{1,0:T(8,128)(2,1)}) custom-call(bf16[256,1792]{1,0:T(8,128)(2,1)S(1)} %copy-done, bf16[256,1024]{1,0:T(8,128)(2,1)S(1)} %copy-done.3, bf16[256,1024]{1,0:T(8,128)(2,1)S(1)} %copy-done.2, bf16[256,1792]{1,0:T(8,128)(2,1)S(1)} %copy-done.1, ...), custom_call_target="tpu_custom_call" | custom-call | tf_op jit(solution)/shard_map/pallas_call | solution.py:462
Async XLA Ops:
  99.3 1.2 %copy-start = (bf16[256,1792]{1,0:T(8,128)(2,1)S(1)}, bf16[256,1792]{1,0:T(8,128)(2,1)}, u32[]{:S(2)}) copy-start(bf16[256,1792]{1,0:T(8,128)(2,1)} %get-tuple-element.17.inputs_ref) | copy-start | bytes 2752516
  100.5 1.2 %copy-start.1 = (bf16[256,1792]{1,0:T(8,128)(2,1)S(1)}, bf16[256,1792]{1,0:T(8,128)(2,1)}, u32[]{:S(2)}) copy-start(bf16[256,1792]{1,0:T(8,128)(2,1)} %get-tuple-element.20.resid_ref) | copy-start | bytes 2752516
  101.7 1.0 copy-start.2
  102.7 1.0 copy-start.3
  103.7 0.8 copy-start.4
  104.6 0.7 copy-start.5
  105.3 0.7 copy-start.6
